TPU v7x, 32 devices: a whole 2x2x4 slice. The times are simulated.
32 devices in a mesh: rep: 4 (over y, x), shard: 8 (over z, core).
Axes of the slice: x: 2, y: 2, z: 4, core: 2. Of those that a mesh axis runs over, the one named last changes fastest.
Arguments:
- queries: bfloat16 [4, 1024, 256], P('rep', 'shard'), may hold values from -64 to 64
- targets: int32 [4, 1024], P('rep', 'shard'), may hold values from 0 to 4095, as said below
- samp_ids: int32 [4, 32], P('rep', 'shard'), may hold values from 0 to 5, as said below
- counts: int32 [4, 8], P('rep', 'shard'), may hold values from 1 to 4, as said below
- logq: float32 [4, 32], P('rep', 'shard'), may hold values from -9 to -5
- table: float32 [6144, 256], P('shard'), may hold values from -1 to 1
- first_moment: float32 [6144, 256], P('shard'), may hold values from -2 to 2
- second_moment: float32 [6144, 256], P('shard'), may hold values from 0.01 to 1
Outputs:
- loss: float32 [4, 1024], P('rep', 'shard')
- query_grad: float32 [4, 1024, 256], P('rep', 'shard')
- new_table: float32 [6144, 256], P('shard')
- new_first: float32 [6144, 256], P('shard')
- new_second: float32 [6144, 256], P('shard')
Inputs may be any that keep to these rules, and one draw needn't show every extreme that they name: In each group some device counts 4; when a device counts 4, the device of its group whose shard index differs in the lowest bit counts at most 2. `samp_ids`: the 4 numbers listed for one device are distinct. `targets`: the slot always lies in a live block of the query's group.
All inputs are finite; a program needn't handle non-finite values.
Results may differ from a plain program's by a relative error of at most 0.0085.
Values may be sent and summed in bfloat16 or wider, within the bound.
A program may use at most 64 MiB of HBM per device.

v0:
```python
import jax
import jax.numpy as jnp
from jax import lax
from jax.sharding import PartitionSpec as P

BLOCK = 128


logit_scale = 2.0
beta_first = 0.9
beta_second = 0.99
learn_rate = 0.01
adam_eps = 1e-08
bias_first = 1.0 - 0.9**10
bias_second = 1.0 - 0.99**10
floor_value = -1e30


def adam_update(weights, first, second, gradient):
    first = beta_first * first + (1.0 - beta_first) * gradient
    second = beta_second * second + (1.0 - beta_second) * gradient * gradient
    weights = weights - learn_rate * (first / bias_first) / (
        jnp.sqrt(second / bias_second) + adam_eps
    )
    return (weights, first, second)


def add_totals(carry, scores, marked, active):
    run_top, run_sum, run_pick = carry
    masked = jnp.where(active, scores, floor_value)
    top = jnp.maximum(run_top, jnp.max(masked, axis=1))
    fresh = jnp.sum(jnp.where(active, jnp.exp(masked - top[:, None]), 0.0), axis=1)
    run_sum = run_sum * jnp.exp(run_top - top) + fresh
    run_pick = run_pick + jnp.sum(jnp.where(marked, scores, 0.0), axis=1)
    return (top, run_sum, run_pick)


def local(queries, targets, samp_ids, counts, logq, table, first_moment, second_moment):
    local_rows = queries.shape[1]
    slot_count = samp_ids.shape[1]
    shard_index = lax.axis_index("shard")
    every_query = lax.all_gather(queries[0], "shard", axis=0, tiled=True)
    every_target = lax.all_gather(targets[0], "shard", axis=0, tiled=True)
    group_rows = every_query.shape[0]
    table_half = table.astype(jnp.bfloat16)
    own_base = shard_index * (slot_count * BLOCK)
    columns = jnp.arange(BLOCK, dtype=jnp.int32)
    block_count = counts[0, 0]
    block_ids = samp_ids[0]
    block_shift = logq[0]

    def score_block(items, shift, base):
        product = lax.dot_general(
            every_query, items, (((1,), (1,)), ((), ())), preferred_element_type=jnp.float32
        )
        scores = logit_scale * product - shift
        marked = (every_target - base)[:, None] == columns[None, :]
        return (scores, marked)

    def local_block(number):
        items = lax.dynamic_slice_in_dim(table_half, block_ids[number] * BLOCK, BLOCK, 0)
        scores, marked = score_block(items, block_shift[number], own_base + number * BLOCK)
        return (items, scores, marked)

    start_carry = (
        jnp.full((group_rows,), floor_value, jnp.float32),
        jnp.zeros((group_rows,), jnp.float32),
        jnp.zeros((group_rows,), jnp.float32),
    )
    carry = start_carry
    for number in range(slot_count):
        first_items, first_scores, first_marked = local_block(number)
        carry = add_totals(carry, first_scores, first_marked, number < block_count)
    run_top, run_sum, run_pick = carry
    top = lax.pmax(run_top, "shard")
    total_sum, picked = lax.psum((run_sum * jnp.exp(run_top - top), run_pick), "shard")
    norm_total = top + jnp.log(total_sum)
    grad_carry = (jnp.zeros(table.shape, jnp.float32), jnp.zeros(every_query.shape, jnp.float32))
    for number in range(slot_count):
        second_gradients, second_query_acc = grad_carry
        second_items, second_scores, second_marked = local_block(number)
        probs = jnp.where(number < block_count, jnp.exp(second_scores - norm_total[:, None]), 0.0)
        dlogit = (probs - second_marked.astype(jnp.float32)).astype(jnp.bfloat16)
        item_part = logit_scale * lax.dot_general(
            dlogit, every_query, (((0,), (0,)), ((), ())), preferred_element_type=jnp.float32
        )
        query_part = logit_scale * jnp.dot(dlogit, second_items, preferred_element_type=jnp.float32)
        second_gradients = lax.dynamic_update_slice_in_dim(
            second_gradients, item_part, block_ids[number] * BLOCK, 0
        )
        grad_carry = (second_gradients, second_query_acc + query_part)
    gradients, query_acc = grad_carry
    query_grad = lax.psum_scatter(query_acc, "shard", scatter_dimension=0, tiled=True)
    own_loss = lax.dynamic_slice_in_dim(norm_total - picked, shard_index * local_rows, local_rows)
    summed = lax.psum(gradients, "rep")
    new_table, new_first, new_second = adam_update(table, first_moment, second_moment, summed)
    return (
        own_loss.reshape(1, local_rows),
        query_grad.reshape(1, local_rows, query_grad.shape[1]),
        new_table,
        new_first,
        new_second,
    )


def solution(mesh):
    in_specs = (
        P("rep", "shard", None),
        P("rep", "shard"),
        P("rep", "shard"),
        P("rep", "shard"),
        P("rep", "shard"),
        P("shard", None),
        P("shard", None),
        P("shard", None),
    )
    out_specs = (
        P("rep", "shard"),
        P("rep", "shard", None),
        P("shard", None),
        P("shard", None),
        P("shard", None),
    )
    return jax.shard_map(local, mesh=mesh, in_specs=in_specs, out_specs=out_specs, check_vma=False)
```

profile of v0, /device:TPU:0, one launch (start us, length us, event | category | flops | bytes accessed | tf_op | source)
XLA Modules:
  0.0 136.6 jit_solution(7034218691416798653)
XLA Ops:
  8.0 1.4 %fusion.44 = (s32[1,1]{1,0:T(1,128)}, s32[1,1]{1,0:T(1,128)}, s32[1,1]{1,0:T(1,128)}, s32[1,1]{1,0:T(1,128)}) fusion(s32[1,4]{1,0:T(1,128)} %param.10), kind=kLoop, calls=%fused_computation.85 | loop fusion | bytes 32 | tf_op jit(solution)/shard_map/slice | solution.py:61
  12.7 0.6 fusion.45
  13.3 16.8 %all-gather = bf16[1,1024,256]{2,1,0:T(8,128)(2,1)S(1)} all-gather(bf16[1,128,256]{2,1,0:T(8,128)(2,1)} %param.8), channel_id=2, replica_groups=mesh['rep'=4,'shard'=8] {'shard'}, dimensions={1}, use_global_device_ids=true | all-gather | bytes 589824 | tf_op jit(solution)/shard_map/all_gather | solution.py:42
  30.1 1.2 convert_element_type.27
  31.3 1.0 select_reduce_fusion.8
  32.4 1.0 select_reduce_fusion.9
  33.3 1.0 select_reduce_fusion.10
  34.3 1.0 select_reduce_fusion.11
  35.3 16.9 %pmax.7 = f32[1024]{0:T(1024)S(1)} all-reduce(f32[1024]{0:T(1024)S(1)} %get-tuple-element.20), channel_id=1, replica_groups=mesh['rep'=4,'shard'=8] {'shard'}, use_global_device_ids=true, to_apply=%region_4.5 | all-reduce | flops 1024 | bytes 8192 | tf_op jit(solution)/shard_map/pmax | solution.py:75
  52.2 8.4 %all-gather.1 = s32[1,1024]{1,0:T(1,128)S(1)} all-gather(s32[1,128]{1,0:T(1,128)S(1)} %copy-done.7), channel_id=3, replica_groups=mesh['rep'=4,'shard'=8] {'shard'}, dimensions={1}, use_global_device_ids=true | all-gather | bytes 4608 | tf_op jit(solution)/shard_map/all_gather | solution.py:43
  60.6 0.3 select_reduce_fusion
  60.9 0.3 select_reduce_fusion.2
  61.3 15.7 %all-reduce = (f32[1024]{0:T(1024)S(1)}, f32[1024]{0:T(1024)S(1)}) all-reduce(f32[1024]{0:T(1024)S(1)} %exponential_multiply_fusion, f32[1024]{0:T(1024)S(1)} %add_add_fusion), channel_id=1, replica_groups=mesh['rep'=4,'shard'=8] {'shard'}, use_global_device_ids=true, to_apply=%region_9.10 | all-reduce | flops 2048 | bytes 16384 | tf_op jit(solution)/shard_map/psum | solution.py:76
  77.4 0.3 fusion.11
  77.7 0.3 fusion.10
  78.3 0.9 copy-done
  79.3 0.3 copy-done.3
  79.6 0.3 fusion.28
  79.9 0.4 convolution_add_fusion.2
  80.3 0.4 convolution_add_fusion.1
  80.7 1.4 fusion
  82.1 0.6 dynamic-slice_bitcast_fusion
  82.7 43.6 %all-reduce.3.cloned.1.call-done = f32[768,256]{1,0:T(8,128)} async-done(((f32[768,256]{1,0:T(8,128)}), f32[768,256]{1,0:T(8,128)}) %all-reduce.3.cloned.1.call-update) | async-done | bytes 786448 | tf_op jit(solution)/shard_map/psum | solution.py:95
  126.3 2.8 %divide_subtract_fusion = (f32[768,256]{1,0:T(8,128)}, f32[768,256]{1,0:T(8,128)}, f32[768,256]{1,0:T(8,128)}) fusion(f32[768,256]{1,0:T(8,128)S(1)} %copy-done.1, f32[768,256]{1,0:T(8,128)} %all-reduce.3.cloned.1.call-done, f32[768,256]{1,0:T(8,128)S(1)} %copy-done.4, f32[768,256]{1,0:T(8,128)S(1)} %copy-done.5), kind=kLoop, calls=%fused_computation.26 | loop fusion | flops 2359296 | bytes 5505024 | tf_op jit(solution)/shard_map/sub | solution.py:22
  (27 shorter events, 0.8 us)
Async XLA Ops:
  8.0 118.3 %all-reduce.3.cloned.1.call-start = ((), (), s32[]{:S(2)}) async-start(), calls=%async_computation.2 | async-start | bytes 1572864 | tf_op jit(solution)/shard_map/psum | solution.py:95
  12.0 0.7 copy-start.6
  31.3 3.0 %copy-start.2 = (bf16[768,256]{1,0:T(8,128)(2,1)}, bf16[768,256]{1,0:T(8,128)(2,1)S(1)}, u32[]{:S(2)}) copy-start(bf16[768,256]{1,0:T(8,128)(2,1)S(1)} %convert_element_type.27) | copy-start | bytes 1179652
  35.3 16.9 %copy-start.7 = (s32[1,128]{1,0:T(1,128)S(1)}, s32[1,128]{1,0:T(1,128)}, u32[]{:S(2)}) copy-start(s32[1,128]{1,0:T(1,128)} %param.9) | copy-start | bytes 1540
  78.3 0.9 copy-start
  78.3 1.3 copy-start.3
  79.2 49.9 %reduce-scatter.2.cloned.1.call-start = ((), (), s32[]{:S(2)}) async-start(), calls=%async_computation.1 | async-start | bytes 1179648 | tf_op jit(solution)/shard_map/reduce_scatter | solution.py:93
  80.7 45.6 %copy-start.4 = (f32[768,256]{1,0:T(8,128)S(1)}, f32[768,256]{1,0:T(8,128)}, u32[]{:S(2)}) copy-start(f32[768,256]{1,0:T(8,128)} %param.14) | copy-start | bytes 2359300
  80.7 45.6 %copy-start.5 = (f32[768,256]{1,0:T(8,128)S(1)}, f32[768,256]{1,0:T(8,128)}, u32[]{:S(2)}) copy-start(f32[768,256]{1,0:T(8,128)} %param.15) | copy-start | bytes 2359300
  82.1 44.2 %copy-start.1 = (f32[768,256]{1,0:T(8,128)S(1)}, f32[768,256]{1,0:T(8,128)}, u32[]{:S(2)}) copy-start(f32[768,256]{1,0:T(8,128)} %param.13) | copy-start | bytes 2359300
Sparse Core Ops, SparseCore 0:
  79.3 46.9 all-reduce.2
Sparse Core Ops, SparseCore 1:
  82.5 30.6 reduce-scatter.1
where the time goes:
time: 137 us
  blocking collectives  57.8 us (42%)
  waiting for transfers between devices  43.7 us (32%)
  between operations  19 us (14%)
  matrix products  7.42 us (5%)
  other arithmetic  4.73 us (3%)
  local copies, waits for them, and re-layouts  3.89 us (3%)
    psum x1, waiting for transfers between devices, local(): summed = lax.psum(gradients, 'rep')  43.6 us
    pmax x1, blocking collectives, local(): top = lax.pmax(run_top, 'shard')  16.9 us
    all_gather x1, blocking collectives, local(): every_query = lax.all_gather(queries[0], 'shard', axis=0, tiled=True)  16.8 us
    psum x1, blocking collectives, local(): lax.psum((run_sum * jnp.exp(run_top - top), run_pick), 'shard')  15.7 us
    all_gather x1, blocking collectives, local(): every_target = lax.all_gather(targets[0], 'shard', axis=0, tiled=True)  8.37 us
    dot_general x4, matrix products, score_block(): lax.dot_general(every_query, items, (((1,), (1,)), ((), ())), preferred_e...  3.88 us
    sub x1, other arithmetic, adam_update(): weights - learn_rate * (first / bias_first) / (jnp.sqrt(second / bias_sec...  2.81 us
  transfers between devices with their start and end apart: 2, of which 1 were waited for; matrix products, arithmetic and copies ran while one was open for 4% of the time, Pallas kernels for 0%

commit v1 on v0

v1 whole, which is shorter than its diff:
```python
import functools

import jax
import jax.numpy as jnp
from jax import lax
from jax.experimental import pallas as pl
from jax.experimental.pallas import tpu as pltpu
from jax.sharding import PartitionSpec as P

BLOCK = 128
MESH = pl.DeviceIdType.MESH

logit_scale = 2.0
beta_first = 0.9
beta_second = 0.99
learn_rate = 0.01
adam_eps = 1e-08
bias_first = 1.0 - 0.9**10
bias_second = 1.0 - 0.99**10
dead_shift = 1e30


def adam_update(weights, first, second, gradient):
    first = beta_first * first + (1.0 - beta_first) * gradient
    second = beta_second * second + (1.0 - beta_second) * gradient * gradient
    weights = weights - learn_rate * (first / bias_first) / (
        jnp.sqrt(second / bias_second) + adam_eps
    )
    return (weights, first, second)


def pick_kernel(slots, blocks, ids_ref, counts_ref, logq_ref, table_ref, mine_ref, shift_ref, place_ref):
    count = counts_ref[0, 0]
    for j in range(slots):
        number = ids_ref[0, j]
        start = pl.multiple_of(number * BLOCK, BLOCK)
        mine_ref[pl.ds(j * BLOCK, BLOCK), :] = table_ref[pl.ds(start, BLOCK), :].astype(jnp.bfloat16)
        shift_ref[j] = jnp.full(shift_ref.shape[1:], jnp.where(j < count, logq_ref[0, j], dead_shift), jnp.float32)
        for b in range(blocks):
            place_ref[b, j] = jnp.full(place_ref.shape[2:], jnp.where(number == b, 1.0, 0.0), jnp.float32)


def kernel(
    n_rep, n_col, slots, blocks,
    targets_ref, queries_ref, mine_ref, shift_ref, place_ref,
    loss_ref, qgrad_ref, grad_ref,
    q_all, t_all, items, items_t, shifts, scores, dlog, stats, norm, pick_own, pick_all,
    part_own, part_out, part_in, qg_own, qg_out, qg_in, bf_out, bf_in,
    q_send, q_recv, t_send, t_recv, it_send, it_recv, st_send, st_recv, pk_send, pk_recv,
    gp_send, gp_recv, qg_send, qg_recv, bf_send, bf_recv,
):
    rep = lax.axis_index("rep")
    shard = lax.axis_index("shard")
    col = shard // 2
    core = shard % 2
    rows = queries_ref.shape[1]
    width = queries_ref.shape[2]
    half_width = width // 2
    half = slots * BLOCK
    bits = n_rep.bit_length() - 1
    sibling = {"rep": rep, "shard": col * 2 + (1 - core)}
    other = 1 - core

    def column(c):
        return {"rep": rep, "shard": c * 2 + core}

    def flipped(bit):
        size = 1 << bit
        return {"rep": rep + size * (1 - 2 * ((rep // size) % 2)), "shard": shard}

    def remote(src, dst, send, recv, device):
        return pltpu.make_async_remote_copy(
            src_ref=src, dst_ref=dst, send_sem=send, recv_sem=recv, device_id=device, device_id_type=MESH
        )

    barrier = pltpu.get_barrier_semaphore()
    for step in range(1, n_col):
        pl.semaphore_signal(barrier, inc=1, device_id=column((col + step) % n_col), device_id_type=MESH)
    pl.semaphore_signal(barrier, inc=1, device_id=sibling, device_id_type=MESH)
    for bit in range(bits):
        pl.semaphore_signal(barrier, inc=1, device_id=flipped(bit), device_id_type=MESH)
    t_all[col] = jnp.broadcast_to(targets_ref[...], (8, rows))
    q_all[col] = queries_ref[0]
    items[core] = mine_ref[...]
    shifts[core] = shift_ref[...]
    pl.semaphore_wait(barrier, n_col + bits)

    for step in range(1, n_col):
        c = (col + step) % n_col
        remote(queries_ref.at[0], q_all.at[col], q_send.at[c], q_recv.at[col], column(c)).start()
        remote(t_all.at[col], t_all.at[col], t_send.at[c], t_recv.at[col], column(c)).start()

    remote(items.at[core], items.at[core], it_send.at[0], it_recv.at[0], sibling).start()
    remote(shifts.at[core], shifts.at[core], it_send.at[1], it_recv.at[1], sibling).start()
    remote(items.at[other], items.at[other], it_send.at[0], it_recv.at[0], sibling).wait_recv()
    remote(shifts.at[other], shifts.at[other], it_send.at[1], it_recv.at[1], sibling).wait_recv()
    for side in range(2):
        items_t[:, pl.ds(side * half, half)] = items[side].T

    row_ids = lax.broadcasted_iota(jnp.int32, (half, rows), 0)
    base = col * (2 * half)

    def score_chunk(c):
        tops = []
        picks = []
        for side in range(2):
            product = lax.dot_general(
                items[side], q_all[c], (((1,), (1,)), ((), ())), preferred_element_type=jnp.float32
            )
            shift = shifts[side][:, None, :, :]
            value = (logit_scale * product).reshape(slots, BLOCK // 8, 8, rows) - shift
            value = value.reshape(half, rows)
            scores[c, side] = value
            marked = row_ids == t_all[c][0:1, :] - (base + side * half)
            tops.append(jnp.max(value, axis=0, keepdims=True))
            picks.append(jnp.sum(jnp.where(marked, value, 0.0), axis=0, keepdims=True))
        top = jnp.maximum(tops[0], tops[1])
        total = jnp.zeros((1, rows), jnp.float32)
        for side in range(2):
            total = total + jnp.sum(jnp.exp(scores[c, side] - top), axis=0, keepdims=True)
        stats[col, pl.ds(c, 1), :] = top
        stats[col, pl.ds(n_col + c, 1), :] = total
        pick_own[c] = jnp.broadcast_to(picks[0] + picks[1], (8, rows))

    score_chunk(col)

    @pl.loop(1, n_col)
    def _(step):
        c = (col + step) % n_col
        remote(q_all.at[c], q_all.at[c], q_send.at[c], q_recv.at[c], sibling).wait_recv()
        remote(t_all.at[c], t_all.at[c], t_send.at[c], t_recv.at[c], sibling).wait_recv()
        score_chunk(c)

    for step in range(1, n_col):
        c = (col + step) % n_col
        remote(stats.at[col], stats.at[col], st_send.at[c], st_recv.at[col], column(c)).start()
    for step in range(1, n_col):
        c = (col + step) % n_col
        remote(pick_own.at[c], pick_all.at[col], pk_send.at[c], pk_recv.at[col], column(c)).start()
    for step in range(1, n_col):
        c = (col + step) % n_col
        remote(stats.at[c], stats.at[c], st_send.at[c], st_recv.at[c], sibling).wait_recv()

    top = stats[0, 0:n_col, :]
    for c in range(1, n_col):
        top = jnp.maximum(top, stats[c, 0:n_col, :])
    total = jnp.zeros_like(top)
    for c in range(n_col):
        total = total + stats[c, n_col : 2 * n_col, :] * jnp.exp(stats[c, 0:n_col, :] - top)
    norm[...] = top + jnp.log(total)

    every_query = q_all[...].reshape(n_col * rows, width)

    def item_part(side):
        @pl.loop(0, n_col)
        def _(c):
            marked = row_ids == t_all[c][0:1, :] - (base + side * half)
            probs = jnp.exp(scores[c, side] - norm[pl.ds(c, 1), :])
            value = (probs - marked.astype(jnp.float32)).astype(jnp.bfloat16)
            dlog[side, :, pl.ds(pl.multiple_of(c * rows, rows), rows)] = value

        return logit_scale * jnp.dot(dlog[side], every_query, preferred_element_type=jnp.float32)

    part_out[...] = item_part(other).astype(jnp.bfloat16)
    to_sibling = remote(
        part_out, part_in, gp_send, gp_recv, sibling
    )
    to_sibling.start()
    part_own[...] = item_part(core)

    def query_part(c):
        lanes = pl.ds(pl.multiple_of(c * rows, rows), rows)
        value = jnp.dot(items_t[:, pl.ds(0, half)], dlog[0, :, lanes], preferred_element_type=jnp.float32)
        value += jnp.dot(items_t[:, pl.ds(half, half)], dlog[1, :, lanes], preferred_element_type=jnp.float32)
        return logit_scale * value

    @pl.loop(1, n_col)
    def _(step):
        c = (col + step) % n_col
        qg_out[c] = query_part(c).astype(jnp.bfloat16)
        remote(qg_out.at[c], qg_in.at[col], qg_send.at[c], qg_recv.at[col], column(c)).start()

    to_sibling.wait_recv()
    part_own[...] = part_own[...] + part_in[...].astype(jnp.float32)
    for b in range(blocks):
        value = jnp.zeros((BLOCK // 8, 8, width), jnp.float32)
        for j in range(slots):
            value = value + place_ref[b, j][None] * part_own[pl.ds(j * BLOCK, BLOCK), :].reshape(BLOCK // 8, 8, width)
        value = value.reshape(BLOCK, width)
        for h in range(2):
            bf_out[0, h, pl.ds(b * BLOCK, BLOCK), :] = value[:, h * half_width : (h + 1) * half_width].astype(
                jnp.bfloat16
            )

    def exchange(stage, h):
        return remote(
            bf_out.at[stage, h], bf_in.at[stage, h], bf_send.at[stage, h], bf_recv.at[stage, h],
            flipped((stage + h) % bits),
        )

    for h in range(2):
        exchange(0, h).start()

    qg_own[...] = query_part(col)
    for stage in range(bits):
        for h in range(2):
            exchange(stage, h).wait_recv()
            value = bf_out[stage, h].astype(jnp.float32) + bf_in[stage, h].astype(jnp.float32)
            if stage + 1 < bits:
                bf_out[stage + 1, h] = value.astype(jnp.bfloat16)
                exchange(stage + 1, h).start()
            else:
                grad_ref[:, h * half_width : (h + 1) * half_width] = value
        if stage == 0:
            total_qg = qg_own[...]
            picked = pick_own[col]
            for step in range(1, n_col):
                c = (col + step) % n_col
                remote(qg_in.at[c], qg_in.at[c], qg_send.at[c], qg_recv.at[c], sibling).wait_recv()
                remote(pick_all.at[c], pick_all.at[c], pk_send.at[c], pk_recv.at[c], sibling).wait_recv()
                total_qg = total_qg + qg_in[c].astype(jnp.float32)
                picked = picked + pick_all[c]
            qgrad_ref[0] = total_qg.T
            loss_ref[...] = norm[pl.ds(col, 1), :] - picked[0:1, :]

    for step in range(1, n_col):
        c = (col + step) % n_col
        remote(q_all.at[col], q_all.at[col], q_send.at[c], q_recv.at[c], sibling).wait_send()
        remote(t_all.at[col], t_all.at[col], t_send.at[c], t_recv.at[c], sibling).wait_send()
        remote(stats.at[col], stats.at[col], st_send.at[c], st_recv.at[c], sibling).wait_send()
        remote(pick_own.at[c], pick_own.at[c], pk_send.at[c], pk_recv.at[c], sibling).wait_send()
        remote(qg_out.at[c], qg_out.at[c], qg_send.at[c], qg_recv.at[c], sibling).wait_send()
    remote(items.at[core], items.at[core], it_send.at[0], it_recv.at[0], sibling).wait_send()
    remote(shifts.at[core], shifts.at[core], it_send.at[1], it_recv.at[1], sibling).wait_send()
    to_sibling.wait_send()
    for stage in range(bits):
        for h in range(2):
            exchange(stage, h).wait_send()


def local(n_rep, n_shard, queries, targets, samp_ids, counts, logq, table, first_moment, second_moment):
    rows, width = queries.shape[1:]
    slots = samp_ids.shape[1]
    items_held = table.shape[0]
    blocks = items_held // BLOCK
    n_col = n_shard // 2
    bits = n_rep.bit_length() - 1
    half = slots * BLOCK
    f32, bf16 = jnp.float32, jnp.bfloat16
    dma = pltpu.SemaphoreType.DMA
    vmem, smem = pl.BlockSpec(memory_space=pltpu.VMEM), pl.BlockSpec(memory_space=pltpu.SMEM)
    pair_flops = n_col * rows * 2 * half * width
    mine, shift, place = pl.pallas_call(
        functools.partial(pick_kernel, slots, blocks),
        out_shape=(
            jax.ShapeDtypeStruct((half, width), bf16),
            jax.ShapeDtypeStruct((slots, 8, BLOCK), f32),
            jax.ShapeDtypeStruct((blocks, slots, 8, width), f32),
        ),
        in_specs=[smem, smem, smem, vmem],
        out_specs=(vmem, vmem, vmem),
        compiler_params=pltpu.CompilerParams(vmem_limit_bytes=16 * 1024 * 1024),
    )(samp_ids, counts, logq, table)
    own_loss, query_grad, gradient = pl.pallas_call(
        functools.partial(kernel, n_rep, n_col, slots, blocks),
        out_shape=(
            jax.ShapeDtypeStruct((1, rows), f32),
            jax.ShapeDtypeStruct((1, rows, width), f32),
            jax.ShapeDtypeStruct((items_held, width), f32),
        ),
        in_specs=[vmem] * 5,
        out_specs=(vmem, vmem, vmem),
        scratch_shapes=[
            pltpu.VMEM((n_col, rows, width), bf16),
            pltpu.VMEM((n_col, 8, rows), jnp.int32),
            pltpu.VMEM((2, half, width), bf16),
            pltpu.VMEM((width, 2 * half), bf16),
            pltpu.VMEM((2, slots, 8, BLOCK), f32),
            pltpu.VMEM((n_col, 2, half, rows), f32),
            pltpu.VMEM((2, half, n_col * rows), bf16),
            pltpu.VMEM((n_col, 2 * n_col, rows), f32),
            pltpu.VMEM((n_col, rows), f32),
            pltpu.VMEM((n_col, 8, rows), f32),
            pltpu.VMEM((n_col, 8, rows), f32),
            pltpu.VMEM((half, width), f32),
            pltpu.VMEM((half, width), bf16),
            pltpu.VMEM((half, width), bf16),
            pltpu.VMEM((width, rows), f32),
            pltpu.VMEM((n_col, width, rows), bf16),
            pltpu.VMEM((n_col, width, rows), bf16),
            pltpu.VMEM((bits, 2, items_held, width // 2), bf16),
            pltpu.VMEM((bits, 2, items_held, width // 2), bf16),
            dma((n_col,)), dma((n_col,)), dma((n_col,)), dma((n_col,)),
            dma((2,)), dma((2,)),
            dma((n_col,)), dma((n_col,)), dma((n_col,)), dma((n_col,)),
            dma(()), dma(()),
            dma((n_col,)), dma((n_col,)),
            dma((bits, 2)), dma((bits, 2)),
        ],
        compiler_params=pltpu.CompilerParams(
            collective_id=0, has_side_effects=True, vmem_limit_bytes=40 * 1024 * 1024
        ),
        cost_estimate=pl.CostEstimate(
            flops=6 * pair_flops, bytes_accessed=4 * items_held * width, transcendentals=2 * pair_flops // width
        ),
    )(targets, queries, mine, shift, place)
    new_table, new_first, new_second = adam_update(table, first_moment, second_moment, gradient)
    return (own_loss, query_grad, new_table, new_first, new_second)


def solution(mesh):
    in_specs = (
        P("rep", "shard", None),
        P("rep", "shard"),
        P("rep", "shard"),
        P("rep", "shard"),
        P("rep", "shard"),
        P("shard", None),
        P("shard", None),
        P("shard", None),
    )
    out_specs = (
        P("rep", "shard"),
        P("rep", "shard", None),
        P("shard", None),
        P("shard", None),
        P("shard", None),
    )
    step = functools.partial(local, mesh.shape["rep"], mesh.shape["shard"])
    return jax.shard_map(step, mesh=mesh, in_specs=in_specs, out_specs=out_specs, check_vma=False)
```

time: 137 us -> 39.4 us (0.29)
  blocking collectives: 57.8 us -> 0 us
  waiting for transfers between devices: 43.7 us -> 0 us
  Pallas kernels: 0 us -> 33.1 us
  between operations: 19 us -> 1.39 us
  matrix products: 7.42 us -> 0 us
  other arithmetic: 4.73 us -> 1.7 us
    psum x1 -> x0, waiting for transfers between devices: 43.6 us -> none  [local(): summed = lax.psum(gradients, 'rep')]
    pallas_call x0 -> x2, Pallas kernels: none -> 33.1 us  [the longest x1 32.6 us: local(): pl.pallas_call(functools.partial(kernel, n_rep, n_col, slots, blocks), ou...]
    all_gather x2 -> x0, blocking collectives: 25.1 us -> none  [the longest x1 16.8 us: local(): every_query = lax.all_gather(queries[0], 'shard', axis=0, tiled=True)]
    pmax x1 -> x0, blocking collectives: 16.9 us -> none  [local(): top = lax.pmax(run_top, 'shard')]
    psum x1 -> x0, blocking collectives: 15.7 us -> none  [local(): lax.psum((run_sum * jnp.exp(run_top - top), run_pick), 'shard')]
    dot_general x12 -> x0, matrix products: 7.42 us -> none  [the longest x4 3.88 us: score_block(): lax.dot_general(every_query, items, (((1,), (1,)), ((), ())), preferred_e...]
    slice x2 -> x0, local copies, waits for them, and re-layouts: 2.01 us -> none  [the longest x1 1.4 us: local_block(): block_ids[number] * BLOCK]
    unnamed x16 -> x18, local copies, waits for them, and re-layouts: 1.24 us -> 2.97 us
  transfers between devices with their start and end apart: 2 -> 0, of which waited for: 1 -> 0; matrix products, arithmetic and copies ran while one was open for 4% -> 0% of each run, Pallas kernels for 0% -> 0%
where the time goes in v1:
time: 39.4 us; the launch traced here: 39.2 us
  Pallas kernels  33.1 us (84%)
  local copies, waits for them, and re-layouts  2.97 us (8%)
  other arithmetic  1.7 us (4%)
  between operations  1.39 us (4%)
    pallas_call x1, Pallas kernels, local(): pl.pallas_call(functools.partial(kernel, n_rep, n_col, slots, blocks), ou...  32.6 us
    unnamed x18, local copies, waits for them, and re-layouts  2.97 us
    sub x1, other arithmetic, adam_update(): weights - learn_rate * (first / bias_first) / (jnp.sqrt(second / bias_sec...  1.7 us

profile of v1, /device:TPU:0, one launch (start us, length us, event | category | flops | bytes accessed | tf_op | source)
XLA Modules:
  0.0 39.2 jit_solution(7287173631546291192)
XLA Ops:
  0.6 0.0 copy-start.3
  0.6 0.0 copy-start.2
  1.3 0.0 copy-done.3
  1.3 0.0 copy-done.2
  1.3 0.0 copy-start
  1.3 1.1 %copy-done = f32[768,256]{1,0:T(8,128)S(1)} copy-done((f32[768,256]{1,0:T(8,128)S(1)}, f32[768,256]{1,0:T(8,128)}, u32[]{:S(2)}) %copy-start) | copy-done | bytes 786456
  2.5 0.0 copy-start.4
  2.5 0.6 %shard_map.119 = (bf16[512,256]{1,0:T(8,128)(2,1)S(1)}, f32[4,8,128]{2,1,0:T(8,128)S(1)}, f32[6,4,8,256]{3,2,1,0:T(8,128)S(1)}) custom-call(s32[1,4]{1,0:T(1,128)S(1)} %copy-done.2, s32[1,1]{1,0:T(1,128)S(6)} %copy.15.counts_ref, f32[1,4]{1,0:T(1,128)S(1)} %copy-done.3, f32[768,256]{1,0:T(8,128)S(1)} %copy-done), custom_call_target="tpu_custom_call" | custom-call | tf_op jit(solution)/shard_map/pallas_call | solution.py:253
  3.1 0.0 copy-start.5
  3.1 0.2 copy-done.4
  3.3 0.4 %copy-done.5 = s32[1,128]{1,0:T(1,128)S(1)} copy-done((s32[1,128]{1,0:T(1,128)S(1)}, s32[1,128]{1,0:T(1,128)}, u32[]{:S(2)}) %copy-start.5) | copy-done | bytes 536
  3.7 0.0 copy-start.1
  3.7 0.0 copy-start.6
  3.7 0.0 copy-start.7
  3.7 32.6 %shard_map.120 = (f32[1,128]{1,0:T(1,128)S(1)}, f32[1,128,256]{2,1,0:T(8,128)S(1)}, f32[768,256]{1,0:T(8,128)S(1)}) custom-call(s32[1,128]{1,0:T(1,128)S(1)} %copy-done.5, bf16[1,128,256]{2,1,0:T(8,128)(2,1)S(1)} %copy-done.4, bf16[512,256]{1,0:T(8,128)(2,1)S(1)} %get-tuple-element.11.mine_ref, f32[4,8,128]{2,1,0:T(8,128)S(1)} %get-tuple-element.12.shift_ref, ...), custom_call_target="tpu_custom_call" | custom-call | flops 805306368 | bytes 786432 | tf_op jit(solution)/shard_map/pallas_call | solution.py:264
  36.3 0.0 copy-done.1
  36.3 0.0 copy-done.6
  36.3 0.0 copy-done.7
  36.3 1.7 %divide_subtract_fusion = (f32[768,256]{1,0:T(8,128)}, f32[768,256]{1,0:T(8,128)}, f32[768,256]{1,0:T(8,128)}) fusion(f32[768,256]{1,0:T(8,128)S(1)} %copy-done.1, f32[768,256]{1,0:T(8,128)S(1)} %get-tuple-element.16, f32[768,256]{1,0:T(8,128)S(1)} %copy-done.6, f32[768,256]{1,0:T(8,128)S(1)} %copy-done.7), kind=kLoop, calls=%fused_computation.2 | loop fusion | flops 2359296 | bytes 5505024 | tf_op jit(solution)/shard_map/sub | solution.py:26
  38.0 0.5 %copy.16 = f32[1,128]{1,0:T(1,128)} copy(f32[1,128]{1,0:T(1,128)S(1)} %get-tuple-element.25) | data formatting | bytes 1024
  38.5 0.7 %copy.17 = f32[1,128,256]{2,1,0:T(8,128)} copy(f32[1,128,256]{2,1,0:T(8,128)S(1)} %get-tuple-element.26) | data formatting | bytes 262144
Async XLA Ops:
  0.6 0.7 %copy-start.3 = (f32[1,4]{1,0:T(1,128)S(1)}, f32[1,4]{1,0:T(1,128)}, u32[]{:S(2)}) copy-start(f32[1,4]{1,0:T(1,128)} %logq_ref.1) | copy-start | bytes 52
  0.6 0.7 %copy-start.2 = (s32[1,4]{1,0:T(1,128)S(1)}, s32[1,4]{1,0:T(1,128)}, u32[]{:S(2)}) copy-start(s32[1,4]{1,0:T(1,128)} %ids_ref.1) | copy-start | bytes 52
  1.3 1.1 %copy-start = (f32[768,256]{1,0:T(8,128)S(1)}, f32[768,256]{1,0:T(8,128)}, u32[]{:S(2)}) copy-start(f32[768,256]{1,0:T(8,128)} %table_ref.1) | copy-start | bytes 2359300
  2.5 0.8 %copy-start.4 = (bf16[1,128,256]{2,1,0:T(8,128)(2,1)S(1)}, bf16[1,128,256]{2,1,0:T(8,128)(2,1)}, u32[]{:S(2)}) copy-start(bf16[1,128,256]{2,1,0:T(8,128)(2,1)} %queries_ref.1) | copy-start | bytes 196612
  3.1 0.7 %copy-start.5 = (s32[1,128]{1,0:T(1,128)S(1)}, s32[1,128]{1,0:T(1,128)}, u32[]{:S(2)}) copy-start(s32[1,128]{1,0:T(1,128)} %targets_ref.1) | copy-start | bytes 1540
  3.7 32.6 %copy-start.1 = (f32[768,256]{1,0:T(8,128)S(1)}, f32[768,256]{1,0:T(8,128)}, u32[]{:S(2)}) copy-start(f32[768,256]{1,0:T(8,128)} %table_ref.1) | copy-start | bytes 2359300
  3.7 32.6 %copy-start.6 = (f32[768,256]{1,0:T(8,128)S(1)}, f32[768,256]{1,0:T(8,128)}, u32[]{:S(2)}) copy-start(f32[768,256]{1,0:T(8,128)} %param.14) | copy-start | bytes 2359300
  3.7 32.6 %copy-start.7 = (f32[768,256]{1,0:T(8,128)S(1)}, f32[768,256]{1,0:T(8,128)}, u32[]{:S(2)}) copy-start(f32[768,256]{1,0:T(8,128)} %param.15) | copy-start | bytes 2359300

commit v2 on v1

--- a/solution.py
+++ b/solution.py
@@ -29,24 +29,13 @@
     return (weights, first, second)
 
 
-def pick_kernel(slots, blocks, ids_ref, counts_ref, logq_ref, table_ref, mine_ref, shift_ref, place_ref):
-    count = counts_ref[0, 0]
-    for j in range(slots):
-        number = ids_ref[0, j]
-        start = pl.multiple_of(number * BLOCK, BLOCK)
-        mine_ref[pl.ds(j * BLOCK, BLOCK), :] = table_ref[pl.ds(start, BLOCK), :].astype(jnp.bfloat16)
-        shift_ref[j] = jnp.full(shift_ref.shape[1:], jnp.where(j < count, logq_ref[0, j], dead_shift), jnp.float32)
-        for b in range(blocks):
-            place_ref[b, j] = jnp.full(place_ref.shape[2:], jnp.where(number == b, 1.0, 0.0), jnp.float32)
-
-
 def kernel(
     n_rep, n_col, slots, blocks,
-    targets_ref, queries_ref, mine_ref, shift_ref, place_ref,
+    ids_ref, counts_ref, logq_ref, targets_ref, queries_ref, table_ref,
     loss_ref, qgrad_ref, grad_ref,
-    q_all, t_all, items, items_t, shifts, scores, dlog, stats, norm, pick_own, pick_all,
+    table_v, id_own, id_in, s_out, s_in, q_all, t_all, items, items_t, shifts, scores, dlog, stats, norm, pick_own, pick_all,
     part_own, part_out, part_in, qg_own, qg_out, qg_in, bf_out, bf_in,
-    q_send, q_recv, t_send, t_recv, it_send, it_recv, st_send, st_recv, pk_send, pk_recv,
+    table_sem, id_send, id_recv, ss_send, ss_recv, q_send, q_recv, t_send, t_recv, it_send, it_recv, st_send, st_recv, pk_send, pk_recv,
     gp_send, gp_recv, qg_send, qg_recv, bf_send, bf_recv,
 ):
     rep = lax.axis_index("rep")
@@ -58,6 +47,8 @@
     half_width = width // 2
     half = slots * BLOCK
     bits = n_rep.bit_length() - 1
+    group = BLOCK * (2 if blocks % 2 == 0 else 1)
+    groups = blocks * BLOCK // group
     sibling = {"rep": rep, "shard": col * 2 + (1 - core)}
     other = 1 - core
 
@@ -72,6 +63,9 @@
         return pltpu.make_async_remote_copy(
             src_ref=src, dst_ref=dst, send_sem=send, recv_sem=recv, device_id=device, device_id_type=MESH
         )
+
+    load_table = pltpu.make_async_copy(table_ref, table_v, table_sem)
+    load_table.start()
 
     barrier = pltpu.get_barrier_semaphore()
     for step in range(1, n_col):
@@ -81,8 +75,11 @@
         pl.semaphore_signal(barrier, inc=1, device_id=flipped(bit), device_id_type=MESH)
     t_all[col] = jnp.broadcast_to(targets_ref[...], (8, rows))
     q_all[col] = queries_ref[0]
-    items[core] = mine_ref[...]
-    shifts[core] = shift_ref[...]
+    count = counts_ref[0, 0]
+    for j in range(slots):
+        shift = jnp.where(j < count, logq_ref[0, j], dead_shift)
+        shifts[core, j] = jnp.full((8, BLOCK), shift, jnp.float32)
+        id_own[j] = jnp.full((8, BLOCK), ids_ref[0, j].astype(jnp.float32), jnp.float32)
     pl.semaphore_wait(barrier, n_col + bits)
 
     for step in range(1, n_col):
@@ -90,6 +87,28 @@
         remote(queries_ref.at[0], q_all.at[col], q_send.at[c], q_recv.at[col], column(c)).start()
         remote(t_all.at[col], t_all.at[col], t_send.at[c], t_recv.at[col], column(c)).start()
 
+    def announce(h):
+        return remote(id_own, id_in.at[h], id_send.at[h], id_recv.at[h], flipped(h % bits))
+
+    for h in range(2):
+        announce(h).start()
+
+    def is_block(tile, b):
+        return jnp.where(tile == float(b), 1.0, 0.0)[None]
+
+    def tiles(value):
+        return value.astype(jnp.float32).reshape(BLOCK // 8, 8, half_width)
+
+    load_table.wait()
+    for j in range(slots):
+        for h in range(2):
+            value = jnp.zeros((BLOCK // 8, 8, half_width), jnp.float32)
+            for b in range(blocks):
+                held = table_v[pl.ds(b * BLOCK, BLOCK), pl.ds(h * half_width, half_width)]
+                value = value + is_block(id_own[j], b) * tiles(held)
+            items[core, pl.ds(j * BLOCK, BLOCK), pl.ds(h * half_width, half_width)] = value.reshape(
+                BLOCK, half_width
+            ).astype(jnp.bfloat16)
     remote(items.at[core], items.at[core], it_send.at[0], it_recv.at[0], sibling).start()
     remote(shifts.at[core], shifts.at[core], it_send.at[1], it_recv.at[1], sibling).start()
     remote(items.at[other], items.at[other], it_send.at[0], it_recv.at[0], sibling).wait_recv()
@@ -151,22 +170,29 @@
 
     every_query = q_all[...].reshape(n_col * rows, width)
 
-    def item_part(side):
+    slot_rows = lax.broadcasted_iota(jnp.int32, (BLOCK, rows), 0)
+
+    def item_part(side, j):
         @pl.loop(0, n_col)
         def _(c):
-            marked = row_ids == t_all[c][0:1, :] - (base + side * half)
-            probs = jnp.exp(scores[c, side] - norm[pl.ds(c, 1), :])
+            marked = slot_rows == t_all[c][0:1, :] - (base + side * half + j * BLOCK)
+            probs = jnp.exp(scores[c, side, pl.ds(j * BLOCK, BLOCK), :] - norm[pl.ds(c, 1), :])
             value = (probs - marked.astype(jnp.float32)).astype(jnp.bfloat16)
-            dlog[side, :, pl.ds(pl.multiple_of(c * rows, rows), rows)] = value
-
-        return logit_scale * jnp.dot(dlog[side], every_query, preferred_element_type=jnp.float32)
-
-    part_out[...] = item_part(other).astype(jnp.bfloat16)
-    to_sibling = remote(
-        part_out, part_in, gp_send, gp_recv, sibling
-    )
-    to_sibling.start()
-    part_own[...] = item_part(core)
+            dlog[side, pl.ds(j * BLOCK, BLOCK), pl.ds(pl.multiple_of(c * rows, rows), rows)] = value
+
+        return logit_scale * jnp.dot(
+            dlog[side, pl.ds(j * BLOCK, BLOCK), :], every_query, preferred_element_type=jnp.float32
+        )
+
+    def to_sibling(j):
+        where = pl.ds(j * BLOCK, BLOCK)
+        return remote(part_out.at[where, :], part_in.at[where, :], gp_send.at[j], gp_recv.at[j], sibling)
+
+    for j in range(slots):
+        part_out[pl.ds(j * BLOCK, BLOCK), :] = item_part(other, j).astype(jnp.bfloat16)
+        to_sibling(j).start()
+    for j in range(slots):
+        part_own[pl.ds(j * BLOCK, BLOCK), :] = item_part(core, j)
 
     def query_part(c):
         lanes = pl.ds(pl.multiple_of(c * rows, rows), rows)
@@ -180,48 +206,71 @@
         qg_out[c] = query_part(c).astype(jnp.bfloat16)
         remote(qg_out.at[c], qg_in.at[col], qg_send.at[c], qg_recv.at[col], column(c)).start()
 
-    to_sibling.wait_recv()
-    part_own[...] = part_own[...] + part_in[...].astype(jnp.float32)
-    for b in range(blocks):
-        value = jnp.zeros((BLOCK // 8, 8, width), jnp.float32)
+    def exchange_slot(h, j):
+        where = pl.ds(j * BLOCK, BLOCK)
+        return remote(
+            s_out.at[h, where, :], s_in.at[h, where, :], ss_send.at[h, j], ss_recv.at[h, j], flipped(h % bits)
+        )
+
+    for j in range(slots):
+        where = pl.ds(j * BLOCK, BLOCK)
+        to_sibling(j).wait_recv()
+        value = part_own[where, :] + part_in[where, :].astype(jnp.float32)
+        for h in range(2):
+            s_out[h, where, :] = value[:, h * half_width : (h + 1) * half_width].astype(jnp.bfloat16)
+            exchange_slot(h, j).start()
+
+    def exchange(stage, h, g):
+        where = pl.ds(g * group, group)
+        return remote(
+            bf_out.at[stage - 1, h, where, :], bf_in.at[stage - 1, h, where, :],
+            bf_send.at[stage - 1, h, g], bf_recv.at[stage - 1, h, g], flipped((stage + h) % bits),
+        )
+
+    def pass_on(stage, h, g, value):
+        if stage < bits:
+            bf_out[stage - 1, h, pl.ds(g * group, group), :] = value.astype(jnp.bfloat16)
+            exchange(stage, h, g).start()
+        else:
+            grad_ref[pl.ds(g * group, group), pl.ds(h * half_width, half_width)] = value
+
+    qg_own[...] = query_part(col)
+    for h in range(2):
+        announce(h).wait_recv()
         for j in range(slots):
-            value = value + place_ref[b, j][None] * part_own[pl.ds(j * BLOCK, BLOCK), :].reshape(BLOCK // 8, 8, width)
-        value = value.reshape(BLOCK, width)
+            exchange_slot(h, j).wait_recv()
+    for g in range(groups):
         for h in range(2):
-            bf_out[0, h, pl.ds(b * BLOCK, BLOCK), :] = value[:, h * half_width : (h + 1) * half_width].astype(
-                jnp.bfloat16
-            )
-
-    def exchange(stage, h):
-        return remote(
-            bf_out.at[stage, h], bf_in.at[stage, h], bf_send.at[stage, h], bf_recv.at[stage, h],
-            flipped((stage + h) % bits),
-        )
-
-    for h in range(2):
-        exchange(0, h).start()
-
-    qg_own[...] = query_part(col)
-    for stage in range(bits):
-        for h in range(2):
-            exchange(stage, h).wait_recv()
-            value = bf_out[stage, h].astype(jnp.float32) + bf_in[stage, h].astype(jnp.float32)
-            if stage + 1 < bits:
-                bf_out[stage + 1, h] = value.astype(jnp.bfloat16)
-                exchange(stage + 1, h).start()
-            else:
-                grad_ref[:, h * half_width : (h + 1) * half_width] = value
-        if stage == 0:
-            total_qg = qg_own[...]
-            picked = pick_own[col]
-            for step in range(1, n_col):
-                c = (col + step) % n_col
-                remote(qg_in.at[c], qg_in.at[c], qg_send.at[c], qg_recv.at[c], sibling).wait_recv()
-                remote(pick_all.at[c], pick_all.at[c], pk_send.at[c], pk_recv.at[c], sibling).wait_recv()
-                total_qg = total_qg + qg_in[c].astype(jnp.float32)
-                picked = picked + pick_all[c]
-            qgrad_ref[0] = total_qg.T
-            loss_ref[...] = norm[pl.ds(col, 1), :] - picked[0:1, :]
+            pieces = []
+            for b in range(g * group // BLOCK, (g + 1) * group // BLOCK):
+                mine = jnp.zeros((BLOCK // 8, 8, half_width), jnp.float32)
+                theirs = mine
+                for j in range(slots):
+                    where = pl.ds(j * BLOCK, BLOCK)
+                    mine = mine + is_block(id_own[j], b) * tiles(s_out[h, where, :])
+                    theirs = theirs + is_block(id_in[h, j], b) * tiles(s_in[h, where, :])
+                pieces.append((mine + theirs).reshape(BLOCK, half_width))
+            pass_on(1, h, g, jnp.concatenate(pieces, axis=0))
+
+    total_qg = qg_own[...]
+    picked = pick_own[col]
+    for step in range(1, n_col):
+        c = (col + step) % n_col
+        remote(qg_in.at[c], qg_in.at[c], qg_send.at[c], qg_recv.at[c], sibling).wait_recv()
+        remote(pick_all.at[c], pick_all.at[c], pk_send.at[c], pk_recv.at[c], sibling).wait_recv()
+        total_qg = total_qg + qg_in[c].astype(jnp.float32)
+        picked = picked + pick_all[c]
+    qgrad_ref[0] = total_qg.T
+    loss_ref[...] = norm[pl.ds(col, 1), :] - picked[0:1, :]
+
+    for stage in range(1, bits):
+        for g in range(groups):
+            for h in range(2):
+                where = pl.ds(g * group, group)
+                exchange(stage, h, g).wait_recv()
+                value = bf_out[stage - 1, h, where, :].astype(jnp.float32)
+                value = value + bf_in[stage - 1, h, where, :].astype(jnp.float32)
+                pass_on(stage + 1, h, g, value)
 
     for step in range(1, n_col):
         c = (col + step) % n_col
@@ -232,10 +281,15 @@
         remote(qg_out.at[c], qg_out.at[c], qg_send.at[c], qg_recv.at[c], sibling).wait_send()
     remote(items.at[core], items.at[core], it_send.at[0], it_recv.at[0], sibling).wait_send()
     remote(shifts.at[core], shifts.at[core], it_send.at[1], it_recv.at[1], sibling).wait_send()
-    to_sibling.wait_send()
-    for stage in range(bits):
-        for h in range(2):
-            exchange(stage, h).wait_send()
+    for j in range(slots):
+        to_sibling(j).wait_send()
+    for h in range(2):
+        announce(h).wait_send()
+        for j in range(slots):
+            exchange_slot(h, j).wait_send()
+        for stage in range(1, bits):
+            for g in range(groups):
+                exchange(stage, h, g).wait_send()
 
 
 def local(n_rep, n_shard, queries, targets, samp_ids, counts, logq, table, first_moment, second_moment):
@@ -250,17 +304,6 @@
     dma = pltpu.SemaphoreType.DMA
     vmem, smem = pl.BlockSpec(memory_space=pltpu.VMEM), pl.BlockSpec(memory_space=pltpu.SMEM)
     pair_flops = n_col * rows * 2 * half * width
-    mine, shift, place = pl.pallas_call(
-        functools.partial(pick_kernel, slots, blocks),
-        out_shape=(
-            jax.ShapeDtypeStruct((half, width), bf16),
-            jax.ShapeDtypeStruct((slots, 8, BLOCK), f32),
-            jax.ShapeDtypeStruct((blocks, slots, 8, width), f32),
-        ),
-        in_specs=[smem, smem, smem, vmem],
-        out_specs=(vmem, vmem, vmem),
-        compiler_params=pltpu.CompilerParams(vmem_limit_bytes=16 * 1024 * 1024),
-    )(samp_ids, counts, logq, table)
     own_loss, query_grad, gradient = pl.pallas_call(
         functools.partial(kernel, n_rep, n_col, slots, blocks),
         out_shape=(
@@ -268,9 +311,14 @@
             jax.ShapeDtypeStruct((1, rows, width), f32),
             jax.ShapeDtypeStruct((items_held, width), f32),
         ),
-        in_specs=[vmem] * 5,
+        in_specs=[smem, smem, smem, vmem, vmem, pl.BlockSpec(memory_space=pl.ANY)],
         out_specs=(vmem, vmem, vmem),
         scratch_shapes=[
+            pltpu.VMEM((items_held, width), f32),
+            pltpu.VMEM((slots, 8, BLOCK), f32),
+            pltpu.VMEM((2, slots, 8, BLOCK), f32),
+            pltpu.VMEM((2, half, width // 2), bf16),
+            pltpu.VMEM((2, half, width // 2), bf16),
             pltpu.VMEM((n_col, rows, width), bf16),
             pltpu.VMEM((n_col, 8, rows), jnp.int32),
             pltpu.VMEM((2, half, width), bf16),
@@ -288,14 +336,15 @@
             pltpu.VMEM((width, rows), f32),
             pltpu.VMEM((n_col, width, rows), bf16),
             pltpu.VMEM((n_col, width, rows), bf16),
-            pltpu.VMEM((bits, 2, items_held, width // 2), bf16),
-            pltpu.VMEM((bits, 2, items_held, width // 2), bf16),
+            pltpu.VMEM((max(bits - 1, 1), 2, items_held, width // 2), bf16),
+            pltpu.VMEM((max(bits - 1, 1), 2, items_held, width // 2), bf16),
+            dma(()), dma((2,)), dma((2,)), dma((2, slots)), dma((2, slots)),
             dma((n_col,)), dma((n_col,)), dma((n_col,)), dma((n_col,)),
             dma((2,)), dma((2,)),
             dma((n_col,)), dma((n_col,)), dma((n_col,)), dma((n_col,)),
-            dma(()), dma(()),
+            dma((slots,)), dma((slots,)),
             dma((n_col,)), dma((n_col,)),
-            dma((bits, 2)), dma((bits, 2)),
+            dma((bits, 2, blocks)), dma((bits, 2, blocks)),
         ],
         compiler_params=pltpu.CompilerParams(
             collective_id=0, has_side_effects=True, vmem_limit_bytes=40 * 1024 * 1024
@@ -303,7 +352,7 @@
         cost_estimate=pl.CostEstimate(
             flops=6 * pair_flops, bytes_accessed=4 * items_held * width, transcendentals=2 * pair_flops // width
         ),
-    )(targets, queries, mine, shift, place)
+    )(samp_ids, counts, logq, targets, queries, table)
     new_table, new_first, new_second = adam_update(table, first_moment, second_moment, gradient)
     return (own_loss, query_grad, new_table, new_first, new_second)
 

time: 39.4 us -> 39.2 us (level)
    pallas_call x1 -> x0, Pallas kernels: 0.58 us -> none  [local(): pl.pallas_call(functools.partial(pick_kernel, slots, blocks), out_shape=(...]
    unnamed x18 -> x16, local copies, waits for them, and re-layouts: 2.97 us -> 3.15 us
where the time goes in v2:
time: 39.2 us; the launch traced here: 39 us
  Pallas kernels  32.8 us (84%)
  local copies, waits for them, and re-layouts  3.15 us (8%)
  other arithmetic  1.69 us (4%)
  between operations  1.39 us (4%)
    pallas_call x1, Pallas kernels, local(): pl.pallas_call(functools.partial(kernel, n_rep, n_col, slots, blocks), ou...  32.8 us
    unnamed x16, local copies, waits for them, and re-layouts  3.15 us
    sub x1, other arithmetic, adam_update(): weights - learn_rate * (first / bias_first) / (jnp.sqrt(second / bias_sec...  1.69 us

profile of v2, /device:TPU:0, one launch (start us, length us, event | category | flops | bytes accessed | tf_op | source)
XLA Modules:
  0.0 39.0 jit_solution(643724857792202643)
XLA Ops:
  0.6 0.0 copy-start.3
  0.6 0.0 copy-start.2
  0.7 0.0 copy-start.4
  1.3 0.0 copy-done.3
  1.3 0.0 copy-done.2
  1.4 0.0 copy-done.4
  1.4 0.0 copy-start
  1.4 1.1 %copy-done = f32[768,256]{1,0:T(8,128)S(1)} copy-done((f32[768,256]{1,0:T(8,128)S(1)}, f32[768,256]{1,0:T(8,128)}, u32[]{:S(2)}) %copy-start) | copy-done | bytes 786456
  2.5 0.0 copy-start.1
  2.5 0.8 %copy-done.1 = bf16[1,128,256]{2,1,0:T(8,128)(2,1)S(1)} copy-done((bf16[1,128,256]{2,1,0:T(8,128)(2,1)S(1)}, bf16[1,128,256]{2,1,0:T(8,128)(2,1)}, u32[]{:S(2)}) %copy-start.1) | copy-done | bytes 65560
  3.3 0.0 copy-start.5
  3.3 0.0 copy-start.6
  3.3 32.8 %shard_map.119 = (f32[1,128]{1,0:T(1,128)S(1)}, f32[1,128,256]{2,1,0:T(8,128)S(1)}, f32[768,256]{1,0:T(8,128)S(1)}) custom-call(s32[1,4]{1,0:T(1,128)S(1)} %copy-done.2, s32[1,1]{1,0:T(1,128)S(6)} %copy.15.counts_ref, f32[1,4]{1,0:T(1,128)S(1)} %copy-done.3, s32[1,128]{1,0:T(1,128)S(1)} %copy-done.4, bf16[1,128,256]{2,1,0:T(8,128)(2,1)S(1)} %copy-done.1, ...), custom_call_target="tpu_custom_call" | custom-call | flops 805306368 | bytes 786432 | tf_op jit(solution)/shard_map/pallas_call | solution.py:307
  36.1 0.0 copy-done.5
  36.1 0.0 copy-done.6
  36.1 1.7 %divide_subtract_fusion = (f32[768,256]{1,0:T(8,128)}, f32[768,256]{1,0:T(8,128)}, f32[768,256]{1,0:T(8,128)}) fusion(f32[768,256]{1,0:T(8,128)S(1)} %copy-done, f32[768,256]{1,0:T(8,128)S(1)} %get-tuple-element.10, f32[768,256]{1,0:T(8,128)S(1)} %copy-done.5, f32[768,256]{1,0:T(8,128)S(1)} %copy-done.6), kind=kLoop, calls=%fused_computation.2 | loop fusion | flops 2359296 | bytes 5505024 | tf_op jit(solution)/shard_map/sub | solution.py:26
  37.8 0.5 %copy.16 = f32[1,128]{1,0:T(1,128)} copy(f32[1,128]{1,0:T(1,128)S(1)} %get-tuple-element.19) | data formatting | bytes 1024
  38.3 0.7 %copy.17 = f32[1,128,256]{2,1,0:T(8,128)} copy(f32[1,128,256]{2,1,0:T(8,128)S(1)} %get-tuple-element.20) | data formatting | bytes 262144
Async XLA Ops:
  0.6 0.7 %copy-start.3 = (f32[1,4]{1,0:T(1,128)S(1)}, f32[1,4]{1,0:T(1,128)}, u32[]{:S(2)}) copy-start(f32[1,4]{1,0:T(1,128)} %logq_ref.1) | copy-start | bytes 52
  0.6 0.7 %copy-start.2 = (s32[1,4]{1,0:T(1,128)S(1)}, s32[1,4]{1,0:T(1,128)}, u32[]{:S(2)}) copy-start(s32[1,4]{1,0:T(1,128)} %ids_ref.1) | copy-start | bytes 52
  0.7 0.7 %copy-start.4 = (s32[1,128]{1,0:T(1,128)S(1)}, s32[1,128]{1,0:T(1,128)}, u32[]{:S(2)}) copy-start(s32[1,128]{1,0:T(1,128)} %targets_ref.1) | copy-start | bytes 1540
  1.4 1.1 %copy-start = (f32[768,256]{1,0:T(8,128)S(1)}, f32[768,256]{1,0:T(8,128)}, u32[]{:S(2)}) copy-start(f32[768,256]{1,0:T(8,128)} %table_ref.1) | copy-start | bytes 2359300
  2.5 0.8 %copy-start.1 = (bf16[1,128,256]{2,1,0:T(8,128)(2,1)S(1)}, bf16[1,128,256]{2,1,0:T(8,128)(2,1)}, u32[]{:S(2)}) copy-start(bf16[1,128,256]{2,1,0:T(8,128)(2,1)} %queries_ref.1) | copy-start | bytes 196612
  3.3 32.8 %copy-start.5 = (f32[768,256]{1,0:T(8,128)S(1)}, f32[768,256]{1,0:T(8,128)}, u32[]{:S(2)}) copy-start(f32[768,256]{1,0:T(8,128)} %param.14) | copy-start | bytes 2359300
  3.3 32.8 %copy-start.6 = (f32[768,256]{1,0:T(8,128)S(1)}, f32[768,256]{1,0:T(8,128)}, u32[]{:S(2)}) copy-start(f32[768,256]{1,0:T(8,128)} %param.15) | copy-start | bytes 2359300

commit v3 on v2

--- a/solution.py
+++ b/solution.py
@@ -31,11 +31,11 @@
 
 def kernel(
     n_rep, n_col, slots, blocks,
-    ids_ref, counts_ref, logq_ref, targets_ref, queries_ref, table_ref,
+    ids_hbm, counts_hbm, logq_hbm, targets_hbm, queries_ref, table_ref,
     loss_ref, qgrad_ref, grad_ref,
-    table_v, id_own, id_in, s_out, s_in, q_all, t_all, items, items_t, shifts, scores, dlog, stats, norm, pick_own, pick_all,
+    ids_ref, counts_ref, logq_ref, targets_ref, table_v, id_own, id_in, s_out, s_in, q_all, t_all, items, items_t, shifts, scores, dlog, stats, norm, pick_own, pick_all,
     part_own, part_out, part_in, qg_own, qg_out, qg_in, bf_out, bf_in,
-    table_sem, id_send, id_recv, ss_send, ss_recv, q_send, q_recv, t_send, t_recv, it_send, it_recv, st_send, st_recv, pk_send, pk_recv,
+    small_sem, own_sem, table_sem, id_send, id_recv, ss_send, ss_recv, q_send, q_recv, t_send, t_recv, it_send, it_recv, st_send, st_recv, pk_send, pk_recv,
     gp_send, gp_recv, qg_send, qg_recv, bf_send, bf_recv,
 ):
     rep = lax.axis_index("rep")
@@ -65,6 +65,16 @@
         )
 
     load_table = pltpu.make_async_copy(table_ref, table_v, table_sem)
+    load_small = [
+        pltpu.make_async_copy(src, dst, small_sem.at[i])
+        for i, (src, dst) in enumerate(
+            [(ids_hbm, ids_ref), (counts_hbm, counts_ref), (logq_hbm, logq_ref), (targets_hbm, targets_ref)]
+        )
+    ]
+    load_own = pltpu.make_async_copy(queries_ref.at[0], q_all.at[col], own_sem)
+    for load in load_small:
+        load.start()
+    load_own.start()
     load_table.start()
 
     barrier = pltpu.get_barrier_semaphore()
@@ -73,8 +83,9 @@
     pl.semaphore_signal(barrier, inc=1, device_id=sibling, device_id_type=MESH)
     for bit in range(bits):
         pl.semaphore_signal(barrier, inc=1, device_id=flipped(bit), device_id_type=MESH)
+    for load in load_small:
+        load.wait()
     t_all[col] = jnp.broadcast_to(targets_ref[...], (8, rows))
-    q_all[col] = queries_ref[0]
     count = counts_ref[0, 0]
     for j in range(slots):
         shift = jnp.where(j < count, logq_ref[0, j], dead_shift)
@@ -141,6 +152,7 @@
         stats[col, pl.ds(n_col + c, 1), :] = total
         pick_own[c] = jnp.broadcast_to(picks[0] + picks[1], (8, rows))
 
+    load_own.wait()
     score_chunk(col)
 
     @pl.loop(1, n_col)
@@ -302,7 +314,7 @@
     half = slots * BLOCK
     f32, bf16 = jnp.float32, jnp.bfloat16
     dma = pltpu.SemaphoreType.DMA
-    vmem, smem = pl.BlockSpec(memory_space=pltpu.VMEM), pl.BlockSpec(memory_space=pltpu.SMEM)
+    vmem = pl.BlockSpec(memory_space=pltpu.VMEM)
     pair_flops = n_col * rows * 2 * half * width
     own_loss, query_grad, gradient = pl.pallas_call(
         functools.partial(kernel, n_rep, n_col, slots, blocks),
@@ -311,9 +323,13 @@
             jax.ShapeDtypeStruct((1, rows, width), f32),
             jax.ShapeDtypeStruct((items_held, width), f32),
         ),
-        in_specs=[smem, smem, smem, vmem, vmem, pl.BlockSpec(memory_space=pl.ANY)],
+        in_specs=[pl.BlockSpec(memory_space=pltpu.HBM)] * 6,
         out_specs=(vmem, vmem, vmem),
         scratch_shapes=[
+            pltpu.SMEM((1, slots), jnp.int32),
+            pltpu.SMEM((1, 1), jnp.int32),
+            pltpu.SMEM((1, slots), f32),
+            pltpu.VMEM((1, rows), jnp.int32),
             pltpu.VMEM((items_held, width), f32),
             pltpu.VMEM((slots, 8, BLOCK), f32),
             pltpu.VMEM((2, slots, 8, BLOCK), f32),
@@ -338,7 +354,7 @@
             pltpu.VMEM((n_col, width, rows), bf16),
             pltpu.VMEM((max(bits - 1, 1), 2, items_held, width // 2), bf16),
             pltpu.VMEM((max(bits - 1, 1), 2, items_held, width // 2), bf16),
-            dma(()), dma((2,)), dma((2,)), dma((2, slots)), dma((2, slots)),
+            dma((4,)), dma(()), dma(()), dma((2,)), dma((2,)), dma((2, slots)), dma((2, slots)),
             dma((n_col,)), dma((n_col,)), dma((n_col,)), dma((n_col,)),
             dma((2,)), dma((2,)),
             dma((n_col,)), dma((n_col,)), dma((n_col,)), dma((n_col,)),
@@ -347,7 +363,7 @@
             dma((bits, 2, blocks)), dma((bits, 2, blocks)),
         ],
         compiler_params=pltpu.CompilerParams(
-            collective_id=0, has_side_effects=True, vmem_limit_bytes=40 * 1024 * 1024
+            collective_id=0, has_side_effects=True, vmem_limit_bytes=60 * 1024 * 1024
         ),
         cost_estimate=pl.CostEstimate(
             flops=6 * pair_flops, bytes_accessed=4 * items_held * width, transcendentals=2 * pair_flops // width

time: 39.2 us -> 39.6 us (1.010)
  local copies, waits for them, and re-layouts: 3.15 us -> 1.85 us
  other arithmetic: 1.69 us -> 2.85 us
  Pallas kernels: 32.8 us -> 33.4 us
    unnamed x16 -> x12, local copies, waits for them, and re-layouts: 3.15 us -> 1.85 us
    sub x1, other arithmetic: 1.69 us -> 2.85 us  [adam_update(): weights - learn_rate * (first / bias_first) / (jnp.sqrt(second / bias_sec...]
    pallas_call x1, Pallas kernels: 32.8 us -> 33.4 us  [local(): pl.pallas_call(functools.partial(kernel, n_rep, n_col, slots, blocks), ou...]
where the time goes in v3:
time: 39.6 us; the launch traced here: 39.4 us
  Pallas kernels  33.4 us (84%)
  other arithmetic  2.85 us (7%)
  local copies, waits for them, and re-layouts  1.85 us (5%)
  between operations  1.35 us (3%)
    pallas_call x1, Pallas kernels, local(): pl.pallas_call(functools.partial(kernel, n_rep, n_col, slots, blocks), ou...  33.4 us
    sub x1, other arithmetic, adam_update(): weights - learn_rate * (first / bias_first) / (jnp.sqrt(second / bias_sec...  2.85 us
    unnamed x12, local copies, waits for them, and re-layouts  1.85 us

profile of v3, /device:TPU:0, one launch (start us, length us, event | category | flops | bytes accessed | tf_op | source)
XLA Modules:
  0.0 39.4 jit_solution(15284560860669543829)
XLA Ops:
  1.3 0.0 copy-start
  1.3 0.0 copy-start.1
  1.3 0.0 copy-start.2
  1.3 33.4 %shard_map.119 = (f32[1,128]{1,0:T(1,128)}, f32[1,128,256]{2,1,0:T(8,128)}, f32[768,256]{1,0:T(8,128)}) custom-call(s32[1,4]{1,0:T(1,128)} %ids_hbm.1, s32[1,1]{1,0:T(1,128)S(6)} %copy.15.counts_hbm, f32[1,4]{1,0:T(1,128)} %logq_hbm.1, s32[1,128]{1,0:T(1,128)} %targets_hbm.1, bf16[1,128,256]{2,1,0:T(8,128)(2,1)} %queries_ref.1, f32[768,256]{1,0:T(8,128)} %table_ref.1), custom_call_target="tpu_custom_call" | custom-call | flops 805306368 | bytes 786432 | tf_op jit(solution)/shard_map/pallas_call | solution.py:319
  34.7 0.0 copy-done
  34.7 0.0 copy-done.1
  34.7 0.0 copy-done.2
  34.7 0.0 copy-start.3
  34.7 2.8 %divide_subtract_fusion = (f32[768,256]{1,0:T(8,128)}, f32[768,256]{1,0:T(8,128)}, f32[768,256]{1,0:T(8,128)}) fusion(f32[768,256]{1,0:T(8,128)S(1)} %copy-done, f32[768,256]{1,0:T(8,128)} %get-tuple-element.10, f32[768,256]{1,0:T(8,128)S(1)} %copy-done.1, f32[768,256]{1,0:T(8,128)S(1)} %copy-done.2), kind=kLoop, calls=%fused_computation.2 | loop fusion | flops 2359296 | bytes 5505024 | tf_op jit(solution)/shard_map/sub | solution.py:26
  37.6 0.0 copy-start.4
  37.6 0.7 %copy-done.4 = f32[1,128]{1,0:T(1,128)S(1)} copy-done((f32[1,128]{1,0:T(1,128)S(1)}, f32[1,128]{1,0:T(1,128)}, u32[]{:S(2)}) %copy-start.4) | copy-done | bytes 536
  38.2 0.5 %copy.16 = f32[1,128]{1,0:T(1,128)} copy(f32[1,128]{1,0:T(1,128)S(1)} %copy-done.4) | data formatting | bytes 1024
  38.8 0.0 copy-done.3
  38.8 0.7 %copy.17 = f32[1,128,256]{2,1,0:T(8,128)} copy(f32[1,128,256]{2,1,0:T(8,128)S(1)} %copy-done.3) | data formatting | bytes 262144
Async XLA Ops:
  1.3 33.4 %copy-start = (f32[768,256]{1,0:T(8,128)S(1)}, f32[768,256]{1,0:T(8,128)}, u32[]{:S(2)}) copy-start(f32[768,256]{1,0:T(8,128)} %table_ref.1) | copy-start | bytes 2359300
  1.3 33.4 %copy-start.1 = (f32[768,256]{1,0:T(8,128)S(1)}, f32[768,256]{1,0:T(8,128)}, u32[]{:S(2)}) copy-start(f32[768,256]{1,0:T(8,128)} %param.14) | copy-start | bytes 2359300
  1.3 33.4 %copy-start.2 = (f32[768,256]{1,0:T(8,128)S(1)}, f32[768,256]{1,0:T(8,128)}, u32[]{:S(2)}) copy-start(f32[768,256]{1,0:T(8,128)} %param.15) | copy-start | bytes 2359300
  34.7 4.0 %copy-start.3 = (f32[1,128,256]{2,1,0:T(8,128)S(1)}, f32[1,128,256]{2,1,0:T(8,128)}, u32[]{:S(2)}) copy-start(f32[1,128,256]{2,1,0:T(8,128)} %get-tuple-element.20) | copy-start | bytes 393220
  37.6 0.7 %copy-start.4 = (f32[1,128]{1,0:T(1,128)S(1)}, f32[1,128]{1,0:T(1,128)}, u32[]{:S(2)}) copy-start(f32[1,128]{1,0:T(1,128)} %get-tuple-element.19) | copy-start | bytes 1540

commit v4 on v3

--- a/solution.py
+++ b/solution.py
@@ -27,6 +27,20 @@
         jnp.sqrt(second / bias_second) + adam_eps
     )
     return (weights, first, second)
+
+
+def finish_kernel(
+    loss_ref, qgrad_ref, grad_ref, table_ref, first_ref, second_ref,
+    loss_out, qgrad_out, table_out, first_out, second_out,
+):
+    @pl.when(pl.program_id(0) == 0)
+    def _():
+        loss_out[...] = loss_ref[...]
+        qgrad_out[...] = qgrad_ref[...]
+
+    table_out[...], first_out[...], second_out[...] = adam_update(
+        table_ref[...], first_ref[...], second_ref[...], grad_ref[...]
+    )
 
 
 def kernel(
@@ -369,8 +383,23 @@
             flops=6 * pair_flops, bytes_accessed=4 * items_held * width, transcendentals=2 * pair_flops // width
         ),
     )(samp_ids, counts, logq, targets, queries, table)
-    new_table, new_first, new_second = adam_update(table, first_moment, second_moment, gradient)
-    return (own_loss, query_grad, new_table, new_first, new_second)
+    tile = BLOCK * (2 if blocks % 2 == 0 else 1)
+    by_tile = pl.BlockSpec((tile, width), lambda i: (i, 0))
+    loss_spec = pl.BlockSpec((1, rows), lambda i: (0, 0))
+    qgrad_spec = pl.BlockSpec((1, rows, width), lambda i: (0, 0, 0))
+    held = jax.ShapeDtypeStruct((items_held, width), f32)
+    return pl.pallas_call(
+        finish_kernel,
+        grid=(items_held // tile,),
+        out_shape=(
+            jax.ShapeDtypeStruct((1, rows), f32),
+            jax.ShapeDtypeStruct((1, rows, width), f32),
+            held, held, held,
+        ),
+        in_specs=[loss_spec, qgrad_spec, by_tile, by_tile, by_tile, by_tile],
+        out_specs=(loss_spec, qgrad_spec, by_tile, by_tile, by_tile),
+        compiler_params=pltpu.CompilerParams(vmem_limit_bytes=60 * 1024 * 1024),
+    )(own_loss, query_grad, gradient, table, first_moment, second_moment)
 
 
 def solution(mesh):

time: 39.6 us -> 39.1 us (0.987)
  Pallas kernels: 33.4 us -> 37.6 us
  other arithmetic: 2.85 us -> 0 us
  local copies, waits for them, and re-layouts: 1.85 us -> 0 us
    pallas_call x0 -> x1, Pallas kernels: none -> 4.23 us  [local(): pl.pallas_call(finish_kernel, grid=(items_held // tile,), out_shape=(jax....]
    sub x1 -> x0, other arithmetic: 2.85 us -> none  [adam_update(): weights - learn_rate * (first / bias_first) / (jnp.sqrt(second / bias_sec...]
    unnamed x12 -> x0, local copies, waits for them, and re-layouts: 1.85 us -> none
where the time goes in v4:
time: 39.1 us; the launch traced here: 38.8 us
  Pallas kernels  37.6 us (96%)
  between operations  1.29 us (3%)
    pallas_call x1, Pallas kernels, local(): pl.pallas_call(functools.partial(kernel, n_rep, n_col, slots, blocks), ou...  33.3 us
    pallas_call x1, Pallas kernels, local(): pl.pallas_call(finish_kernel, grid=(items_held // tile,), out_shape=(jax....  4.23 us

profile of v4, /device:TPU:0, one launch (start us, length us, event | category | flops | bytes accessed | tf_op | source)
XLA Modules:
  0.0 38.8 jit_solution(1676038719440207459)
XLA Ops:
  1.3 33.3 %shard_map.119 = (f32[1,128]{1,0:T(1,128)}, f32[1,128,256]{2,1,0:T(8,128)}, f32[768,256]{1,0:T(8,128)}) custom-call(s32[1,4]{1,0:T(1,128)} %ids_hbm.1, s32[1,1]{1,0:T(1,128)S(6)} %copy.13.counts_hbm, f32[1,4]{1,0:T(1,128)} %logq_hbm.1, s32[1,128]{1,0:T(1,128)} %targets_hbm.1, bf16[1,128,256]{2,1,0:T(8,128)(2,1)} %queries_ref.1, f32[768,256]{1,0:T(8,128)} %table_ref.3), custom_call_target="tpu_custom_call" | custom-call | flops 805306368 | bytes 786432 | tf_op jit(solution)/shard_map/pallas_call | solution.py:333
  34.6 4.2 %shard_map.120 = (f32[1,128]{1,0:T(1,128)}, f32[1,128,256]{2,1,0:T(8,128)}, f32[768,256]{1,0:T(8,128)}, f32[768,256]{1,0:T(8,128)}, f32[768,256]{1,0:T(8,128)}) custom-call(f32[1,128]{1,0:T(1,128)} %get-tuple-element.8.loss_ref, f32[1,128,256]{2,1,0:T(8,128)} %get-tuple-element.9.qgrad_ref, f32[768,256]{1,0:T(8,128)} %get-tuple-element.10.grad_ref, ...), custom_call_target="tpu_custom_call" | custom-call | tf_op jit(solution)/shard_map/pallas_call | solution.py:391

commit v5 on v4

--- a/solution.py
+++ b/solution.py
@@ -383,7 +383,7 @@
             flops=6 * pair_flops, bytes_accessed=4 * items_held * width, transcendentals=2 * pair_flops // width
         ),
     )(samp_ids, counts, logq, targets, queries, table)
-    tile = BLOCK * (2 if blocks % 2 == 0 else 1)
+    tile = BLOCK
     by_tile = pl.BlockSpec((tile, width), lambda i: (i, 0))
     loss_spec = pl.BlockSpec((1, rows), lambda i: (0, 0))
     qgrad_spec = pl.BlockSpec((1, rows, width), lambda i: (0, 0, 0))

time: 39.1 us -> 40.2 us (1.028)
  Pallas kernels: 37.6 us -> 38.7 us
    pallas_call x1, Pallas kernels: 4.23 us -> 5.37 us  [local(): pl.pallas_call(finish_kernel, grid=(items_held // tile,), out_shape=(jax....]
where the time goes in v5:
time: 40.2 us; the launch traced here: 40 us
  Pallas kernels  38.7 us (96%)
  between operations  1.29 us (3%)
    pallas_call x1, Pallas kernels, local(): pl.pallas_call(functools.partial(kernel, n_rep, n_col, slots, blocks), ou...  33.3 us
    pallas_call x1, Pallas kernels, local(): pl.pallas_call(finish_kernel, grid=(items_held // tile,), out_shape=(jax....  5.37 us

profile of v5, /device:TPU:0, one launch (start us, length us, event | category | flops | bytes accessed | tf_op | source)
XLA Modules:
  0.0 40.0 jit_solution(7835483437612847389)
XLA Ops:
  1.3 33.3 %shard_map.119 = (f32[1,128]{1,0:T(1,128)}, f32[1,128,256]{2,1,0:T(8,128)}, f32[768,256]{1,0:T(8,128)}) custom-call(s32[1,4]{1,0:T(1,128)} %ids_hbm.1, s32[1,1]{1,0:T(1,128)S(6)} %copy.13.counts_hbm, f32[1,4]{1,0:T(1,128)} %logq_hbm.1, s32[1,128]{1,0:T(1,128)} %targets_hbm.1, bf16[1,128,256]{2,1,0:T(8,128)(2,1)} %queries_ref.1, f32[768,256]{1,0:T(8,128)} %table_ref.3), custom_call_target="tpu_custom_call" | custom-call | flops 805306368 | bytes 786432 | tf_op jit(solution)/shard_map/pallas_call | solution.py:333
  34.6 5.4 %shard_map.120 = (f32[1,128]{1,0:T(1,128)}, f32[1,128,256]{2,1,0:T(8,128)}, f32[768,256]{1,0:T(8,128)}, f32[768,256]{1,0:T(8,128)}, f32[768,256]{1,0:T(8,128)}) custom-call(f32[1,128]{1,0:T(1,128)} %get-tuple-element.8.loss_ref, f32[1,128,256]{2,1,0:T(8,128)} %get-tuple-element.9.qgrad_ref, f32[768,256]{1,0:T(8,128)} %get-tuple-element.10.grad_ref, ...), custom_call_target="tpu_custom_call" | custom-call | tf_op jit(solution)/shard_map/pallas_call | solution.py:391

commit v6 on v5

--- a/solution.py
+++ b/solution.py
@@ -383,7 +383,7 @@
             flops=6 * pair_flops, bytes_accessed=4 * items_held * width, transcendentals=2 * pair_flops // width
         ),
     )(samp_ids, counts, logq, targets, queries, table)
-    tile = BLOCK
+    tile = items_held // (2 if blocks % 2 == 0 else 1)
     by_tile = pl.BlockSpec((tile, width), lambda i: (i, 0))
     loss_spec = pl.BlockSpec((1, rows), lambda i: (0, 0))
     qgrad_spec = pl.BlockSpec((1, rows, width), lambda i: (0, 0, 0))

time: 40.2 us -> 37.9 us (0.943)
  Pallas kernels: 38.7 us -> 36.5 us
    pallas_call x1, Pallas kernels: 5.37 us -> 3.16 us  [local(): pl.pallas_call(finish_kernel, grid=(items_held // tile,), out_shape=(jax....]
where the time goes in v6:
time: 37.9 us; the launch traced here: 37.8 us
  Pallas kernels  36.5 us (96%)
  between operations  1.29 us (3%)
    pallas_call x1, Pallas kernels, local(): pl.pallas_call(functools.partial(kernel, n_rep, n_col, slots, blocks), ou...  33.3 us
    pallas_call x1, Pallas kernels, local(): pl.pallas_call(finish_kernel, grid=(items_held // tile,), out_shape=(jax....  3.16 us

profile of v6, /device:TPU:0, one launch (start us, length us, event | category | flops | bytes accessed | tf_op | source)
XLA Modules:
  0.0 37.8 jit_solution(17282440809847733199)
XLA Ops:
  1.3 33.3 %shard_map.119 = (f32[1,128]{1,0:T(1,128)}, f32[1,128,256]{2,1,0:T(8,128)}, f32[768,256]{1,0:T(8,128)}) custom-call(s32[1,4]{1,0:T(1,128)} %ids_hbm.1, s32[1,1]{1,0:T(1,128)S(6)} %copy.13.counts_hbm, f32[1,4]{1,0:T(1,128)} %logq_hbm.1, s32[1,128]{1,0:T(1,128)} %targets_hbm.1, bf16[1,128,256]{2,1,0:T(8,128)(2,1)} %queries_ref.1, f32[768,256]{1,0:T(8,128)} %table_ref.3), custom_call_target="tpu_custom_call" | custom-call | flops 805306368 | bytes 786432 | tf_op jit(solution)/shard_map/pallas_call | solution.py:333
  34.6 3.2 %shard_map.120 = (f32[1,128]{1,0:T(1,128)}, f32[1,128,256]{2,1,0:T(8,128)}, f32[768,256]{1,0:T(8,128)}, f32[768,256]{1,0:T(8,128)}, f32[768,256]{1,0:T(8,128)}) custom-call(f32[1,128]{1,0:T(1,128)} %get-tuple-element.8.loss_ref, f32[1,128,256]{2,1,0:T(8,128)} %get-tuple-element.9.qgrad_ref, f32[768,256]{1,0:T(8,128)} %get-tuple-element.10.grad_ref, ...), custom_call_target="tpu_custom_call" | custom-call | tf_op jit(solution)/shard_map/pallas_call | solution.py:391
